TPU v7x, 32 devices: a whole 2x2x4 slice. The times are simulated.
32 devices in a mesh: expert: 4 (over y, x), seq: 8 (over z, core).
Axes of the slice: x: 2, y: 2, z: 4, core: 2. Of those that a mesh axis runs over, the one named last changes fastest.
Arguments:
- moe_input: bfloat16 [8, 256, 2048], P('seq', 'expert'), may hold values from -6 to 6
- out_grad: bfloat16 [8, 256, 2048], P('seq', 'expert'), may hold values from -6 to 6
- expert_id: int32 [8, 256, 1], P('seq', 'expert'), may hold values from 0 to 7; in each aligned block of 64 rows (0 to 63, 64 to 127, ..., all dimensions but the last counted through in order) at most 10 rows name the same one
- w_gate: bfloat16 [8, 2048, 8192], P('expert', None, 'seq'), may hold values from -0.125 to 0.125
- w_up: bfloat16 [8, 2048, 8192], P('expert', None, 'seq'), may hold values from -0.125 to 0.125
- w_down: bfloat16 [8, 8192, 2048], P('expert', 'seq'), may hold values from -0.0625 to 0.0625
- w_out: bfloat16 [4096, 2048], P('expert'), may hold values from -0.09375 to 0.09375
- b_proj: bfloat16 [8, 256, 128], P('seq'), may hold values from -6 to 6
- c_proj: bfloat16 [8, 256, 128], P('seq'), may hold values from -0.046875 to 0.046875
- log_decay: float32 [8, 64, 256], P('seq', 'expert'), may hold values from -0.7 to 0, as said below
Outputs:
- head_grad: bfloat16 [8, 256, 4096], P('seq', None, 'expert')
- input_grad: bfloat16 [8, 256, 2048], P('seq', 'expert')
- gate_grad: float32 [8, 2048, 8192], P('expert', None, 'seq')
- up_grad: float32 [8, 2048, 8192], P('expert', None, 'seq')
- down_grad: float32 [8, 8192, 2048], P('expert', 'seq')
Inputs may be any that keep to these rules, and one draw needn't show every extreme that they name: `expert_id`: at most 10 tokens of one aligned block of 64 tokens (one device's tokens) name the same expert, and some block reaches 10. `log_decay`: Negative.
All inputs are finite; a program needn't handle non-finite values.
Results may differ from a plain program's by a relative error of at most 0.019.
Values may be sent and summed in bfloat16 or wider, within the bound.
A program may use at most 192 MiB of HBM per device.

v0:
```python
import jax
import jax.numpy as jnp
from jax import lax
from jax.experimental import pallas as pl
from jax.experimental.pallas import tpu as pltpu
from jax.sharding import PartitionSpec as P

P_SIZE = 64
CAP = 10
VMEM = 60 * 1024 * 1024
NN = (((1,), (0,)), ((), ()))
NT = (((1,), (1,)), ((), ()))
TN = (((0,), (0,)), ((), ()))


def mm(a, b, dims):
    return lax.dot_general(a, b, dims, preferred_element_type=jnp.float32)


def terms_kernel(x_ref, dy_ref, wg_ref, wu_ref, wd_ref, h_ref, g_ref, u_ref, back_ref, acc):
    step = pl.program_id(0)
    x = x_ref[...]
    gate = mm(x, wg_ref[0], NN)
    up = mm(x, wu_ref[0], NN)
    grad = mm(dy_ref[...], wd_ref[0], NT)
    logistic = jax.nn.sigmoid(gate)
    activated = gate * logistic
    h_ref[...] = (activated * up).astype(jnp.bfloat16)
    up_term = (grad * activated).astype(jnp.bfloat16)
    gate_term = (grad * up * logistic * (1.0 + gate * (1.0 - logistic))).astype(jnp.bfloat16)
    g_ref[...] = gate_term
    u_ref[...] = up_term
    part = mm(gate_term, wg_ref[0], NT) + mm(up_term, wu_ref[0], NT)

    @pl.when(step == 0)
    def _():
        acc[...] = part

    @pl.when(step > 0)
    def _():
        acc[...] += part

    @pl.when(step == pl.num_programs(0) - 1)
    def _():
        back_ref[...] = acc[...].astype(jnp.bfloat16)


def expert_terms(e, x, dy, w_gate, w_up, w_down):
    rows, width = x.shape
    hidden = w_gate.shape[2]
    tile = min(256, hidden)
    whole = pl.BlockSpec((rows, width), lambda i: (0, 0))
    part = pl.BlockSpec((rows, tile), lambda i: (0, i))
    column = pl.BlockSpec((1, width, tile), lambda i: (e, 0, i))
    row = pl.BlockSpec((1, tile, width), lambda i: (e, i, 0))
    term = jax.ShapeDtypeStruct((rows, hidden), jnp.bfloat16)
    return pl.pallas_call(
        terms_kernel,
        grid=(hidden // tile,),
        in_specs=[whole, whole, column, column, row],
        out_specs=[part, part, part, whole],
        out_shape=[term, term, term, jax.ShapeDtypeStruct((rows, width), jnp.bfloat16)],
        scratch_shapes=[pltpu.VMEM((rows, width), jnp.float32)],
        compiler_params=pltpu.CompilerParams(vmem_limit_bytes=VMEM),
        cost_estimate=pl.CostEstimate(
            flops=10 * rows * width * hidden,
            bytes_accessed=6 * width * hidden + 6 * rows * width,
            transcendentals=rows * hidden,
        ),
        name="expert_terms",
    )(x, dy, w_gate, w_up, w_down)


def weight_grads(e, count, left, rights, held):
    rows, width = left.shape
    breadth = rights[0].shape[1]
    tile = min(256, width)
    number = len(rights)

    def kernel(*refs):
        left_ref, right_refs, out_refs = refs[0], refs[1 : 1 + number], refs[-number:]
        for right_ref, out_ref in zip(right_refs, out_refs):
            out_ref[0] = mm(left_ref[...], right_ref[...], TN)

    out = pl.BlockSpec((1, tile, breadth), lambda i: (e, i, 0))
    kept = [] if held is None else list(held)
    return pl.pallas_call(
        kernel,
        grid=(width // tile,),
        in_specs=[pl.BlockSpec((rows, tile), lambda i: (0, i))]
        + [pl.BlockSpec((rows, breadth), lambda i: (0, 0))] * number
        + [pl.BlockSpec(memory_space=pl.ANY)] * len(kept),
        out_specs=[out] * number,
        out_shape=[jax.ShapeDtypeStruct((count, width, breadth), jnp.float32)] * number,
        input_output_aliases={1 + number + k: k for k in range(len(kept))},
        compiler_params=pltpu.CompilerParams(vmem_limit_bytes=VMEM),
        cost_estimate=pl.CostEstimate(
            flops=2 * number * rows * width * breadth,
            bytes_accessed=4 * number * width * breadth,
            transcendentals=0,
        ),
        name="weight_grads",
    )(left, *rights, *kept)


def body(moe_input, out_grad, expert_id, w_gate, w_up, w_down, w_out, b_proj, c_proj, log_decay):
    groups = lax.axis_size("expert")
    group = lax.axis_index("expert")
    shards = lax.axis_size("seq")
    shard = lax.axis_index("seq")
    local = w_gate.shape[0]
    tokens, width = moe_input.shape[1:]
    heads = w_out.shape[0] // P_SIZE
    lanes = heads * P_SIZE
    length, state = b_proj.shape[1:]
    bf = jnp.bfloat16

    labelled = jnp.concatenate(
        [moe_input[0], jnp.broadcast_to(expert_id[0], (tokens, 128)).astype(bf)], axis=1
    )
    x_all = lax.all_gather(labelled, "expert", axis=0, tiled=True)
    dy_all = lax.all_gather(out_grad[0], "expert", axis=0, tiled=True)
    labels = x_all[:, width].astype(jnp.int32)
    x_all = x_all[:, :width]
    here = jnp.arange(length, dtype=jnp.int32)
    same = (
        (labels[:, None] == labels[None, :])
        & (here[:, None] // tokens == here[None, :] // tokens)
        & (here[None, :] < here[:, None])
    )
    slot = jnp.sum(same.astype(jnp.int32), axis=1)
    place = (here // tokens) * CAP + slot
    span = groups * CAP

    xs, dys = [], []
    for e in range(local):
        mine = jnp.where(labels == group * local + e, place, -1)
        pick = (jnp.arange(span, dtype=jnp.int32)[:, None] == mine[None, :]).astype(bf)
        xs.append(mm(pick, x_all, NN).astype(bf))
        dys.append(mm(pick, dy_all, NN).astype(bf))
    gathered = [
        [lax.all_gather(part, "seq", axis=0, tiled=True) for part in (xs[e], dys[e])]
        for e in range(local)
    ]

    gate_up, down, returned = None, None, []
    for e in range(local):
        x, dy = gathered[e]
        hidden, gate_term, up_term, back = expert_terms(e, x, dy, w_gate, w_up, w_down)
        summed = lax.psum_scatter(back, "seq", scatter_dimension=0, tiled=True)
        returned.append(lax.all_gather(summed, "expert", axis=0, tiled=True))
        gate_up = weight_grads(e, local, x, [gate_term, up_term], gate_up)
        down = weight_grads(e, local, hidden, [dy], down)

    expert_all = 0.0
    for e in range(local):
        row = jnp.where(labels % local == e, (labels // local) * span + place, -1)
        take = (row[:, None] == jnp.arange(groups * span, dtype=jnp.int32)[None, :]).astype(bf)
        expert_all = expert_all + mm(take, returned[e], NN)
    expert_all = expert_all.astype(bf)
    own = lax.dynamic_slice_in_dim(expert_all, group * tokens, tokens, axis=0)
    input_grad = (out_grad[0].astype(jnp.float32) + own.astype(jnp.float32)).astype(bf)

    acum = jnp.cumsum(log_decay[0], axis=1)
    b_rows, c_rows = b_proj[0], c_proj[0]
    wide = jnp.repeat(acum.T, P_SIZE, axis=1)
    grow = jnp.exp(wide)
    tail = jnp.exp(wide[-1:] - wide)
    total = grow[-1:]
    high = total.astype(bf)
    low = (total - high.astype(jnp.float32)).astype(bf)
    later = here[:, None] >= here[None, :]
    scores = jnp.where(later, mm(c_rows, b_rows, NT), 0.0)
    difference = jnp.where(later[None], acum[:, :, None] - acum[:, None, :], 0.0)
    weight = (jnp.exp(difference) * scores[None]).astype(bf)

    head_out = mm(dy_all, w_out, NT) + mm(expert_all, w_out, NT)
    summary = mm(c_rows, (grow * head_out).astype(bf), TN).astype(bf)
    sent = jnp.concatenate([summary, high, low, jnp.zeros((14, lanes), bf)], axis=0)
    states = lax.all_gather(sent, "seq", axis=0, tiled=False)
    local_part = jnp.einsum(
        "hts,thp->shp",
        weight,
        head_out.astype(bf).reshape(length, heads, P_SIZE),
        preferred_element_type=jnp.float32,
    ).reshape(length, lanes)
    carried = jnp.zeros((state, lanes), jnp.float32)
    factor = jnp.ones((1, lanes), jnp.float32)
    for r in range(shards):
        after = r > shard
        carried = carried + jnp.where(after, factor, 0.0) * states[r, :state].astype(jnp.float32)
        whole = states[r, state : state + 1].astype(jnp.float32) + states[
            r, state + 1 : state + 2
        ].astype(jnp.float32)
        factor = jnp.where(after, factor * whole, factor)
    cross = tail * mm(b_rows, carried.astype(bf), NN)
    head_grad = (local_part + cross).astype(bf)
    return (head_grad[None], input_grad[None], gate_up[0], gate_up[1], down[0])


def solution(mesh):
    return jax.shard_map(
        body,
        mesh=mesh,
        in_specs=(
            P("seq", "expert", None),
            P("seq", "expert", None),
            P("seq", "expert", None),
            P("expert", None, "seq"),
            P("expert", None, "seq"),
            P("expert", "seq", None),
            P("expert", None),
            P("seq", None, None),
            P("seq", None, None),
            P("seq", "expert", None),
        ),
        out_specs=(
            P("seq", None, "expert"),
            P("seq", "expert", None),
            P("expert", None, "seq"),
            P("expert", None, "seq"),
            P("expert", "seq", None),
        ),
        check_vma=False,
    )
```

profile of v0, /device:TPU:0, one launch (start us, length us, event | category | flops | bytes accessed | tf_op | source)
XLA Modules:
  0.0 304.2 jit_solution(5440206108319035418)
XLA Ops:
  7.2 0.0 all-gather.10.cloned.1.call-start
  7.2 0.7 convert_bitcast_fusion
  7.9 0.1 broadcast_in_dim.76
  8.0 1.7 pad_maximum_fusion
  9.6 0.0 all-gather.10.cloned.1.call-update
  9.7 0.0 all-gather.20.cloned.1.call-start
  9.7 0.7 all-gather.20.cloned.1.call-update
  10.4 0.0 all-gather.12.cloned.1.call-start
  10.5 29.9 %all-gather.10.cloned.1.call-done = bf16[256,2176]{1,0:T(8,128)(2,1)} async-done(((bf16[64,2176]{1,0:T(8,128)(2,1)}), bf16[256,2176]{1,0:T(8,128)(2,1)}) %all-gather.10.cloned.1.call-update) | async-done | bytes 1114128 | tf_op jit(solution)/shard_map/all_gather | solution.py:121
  40.3 0.8 slice.117
  41.2 0.1 copy.48
  41.3 0.2 convert_reduce_fusion
  41.5 2.2 convolution_convert_fusion.3
  43.7 0.0 all-gather.12.cloned.1.call-update
  43.7 0.0 all-gather.14.cloned.1.call-start
  43.8 25.0 %all-gather.20.cloned.1.call-done = bf16[1,256,2048]{2,1,0:T(8,128)(2,1)} async-done(((bf16[1,64,2048]{2,1,0:T(8,128)(2,1)}), bf16[1,256,2048]{2,1,0:T(8,128)(2,1)}) %all-gather.20.cloned.1.call-update) | async-done | bytes 1048592 | tf_op jit(solution)/shard_map/all_gather | solution.py:122
  68.8 2.2 convolution_convert_fusion.2
  71.0 0.0 all-gather.14.cloned.1.call-update
  71.0 0.0 all-gather.16.cloned.1.call-start
  71.1 2.2 convolution_convert_fusion.1
  73.3 0.0 all-gather.18.cloned.1.call-start
  73.4 2.2 convolution_convert_fusion
  75.6 0.0 reduce-scatter.3.cloned.1.call-start
  75.6 18.9 %all-gather.12.cloned.1.call-done.x_ref.refs_0_ = bf16[320,2048]{1,0:T(8,128)(2,1)} async-done(((bf16[40,2048]{1,0:T(8,128)(2,1)}), bf16[320,2048]{1,0:T(8,128)(2,1)}) %all-gather.12.cloned.1.call-update) | async-done | bytes 1310736 | tf_op jit(solution)/shard_map/all_gather | solution.py:142
  94.5 25.0 %all-gather.14.cloned.1.call-done.dy_ref.refs_1_ = bf16[320,2048]{1,0:T(8,128)(2,1)} async-done(((bf16[40,2048]{1,0:T(8,128)(2,1)}), bf16[320,2048]{1,0:T(8,128)(2,1)}) %all-gather.14.cloned.1.call-update) | async-done | bytes 1310736 | tf_op jit(solution)/shard_map/all_gather | solution.py:142
  119.6 18.6 %expert_terms.2 = (bf16[320,1024]{1,0:T(8,128)(2,1)}, bf16[320,1024]{1,0:T(8,128)(2,1)}, bf16[320,1024]{1,0:T(8,128)(2,1)}, bf16[320,2048]{1,0:T(8,128)(2,1)}) custom-call(bf16[320,2048]{1,0:T(8,128)(2,1)} %all-gather.12.cloned.1.call-done.x_ref.refs_0_, bf16[320,2048]{1,0:T(8,128)(2,1)} %all-gather.14.cloned.1.call-done.dy_ref.refs_1_, ...), custom_call_target="tpu_custom_call" | custom-call | flops 6710886400 | bytes 16515072 | tf_op jit(solution)/shard_map/expert_terms/pallas_call | solution.py:57
  138.1 0.0 reduce-scatter.3.cloned.1.call-update
  138.2 0.0 reduce-scatter.5.cloned.1.call-start
  138.2 6.4 %all-gather.16.cloned.1.call-done.x_ref.refs_0_ = bf16[320,2048]{1,0:T(8,128)(2,1)} async-done(((bf16[40,2048]{1,0:T(8,128)(2,1)}), bf16[320,2048]{1,0:T(8,128)(2,1)}) %all-gather.16.cloned.1.call-update) | async-done | bytes 1310736 | tf_op jit(solution)/shard_map/all_gather | solution.py:142
  144.6 25.0 %all-gather.18.cloned.1.call-done.dy_ref.refs_1_ = bf16[320,2048]{1,0:T(8,128)(2,1)} async-done(((bf16[40,2048]{1,0:T(8,128)(2,1)}), bf16[320,2048]{1,0:T(8,128)(2,1)}) %all-gather.18.cloned.1.call-update) | async-done | bytes 1310736 | tf_op jit(solution)/shard_map/all_gather | solution.py:142
  169.6 18.5 %expert_terms.3 = (bf16[320,1024]{1,0:T(8,128)(2,1)}, bf16[320,1024]{1,0:T(8,128)(2,1)}, bf16[320,1024]{1,0:T(8,128)(2,1)}, bf16[320,2048]{1,0:T(8,128)(2,1)}) custom-call(bf16[320,2048]{1,0:T(8,128)(2,1)} %all-gather.16.cloned.1.call-done.x_ref.refs_0_, bf16[320,2048]{1,0:T(8,128)(2,1)} %all-gather.18.cloned.1.call-done.dy_ref.refs_1_, ...), custom_call_target="tpu_custom_call" | custom-call | flops 6710886400 | bytes 16515072 | tf_op jit(solution)/shard_map/expert_terms/pallas_call | solution.py:57
  188.1 0.0 reduce-scatter.5.cloned.1.call-update
  188.1 0.0 all-gather.22.cloned.1.call-start
  188.2 0.6 reduce-window.6
  188.8 0.2 slice_reduce_fusion
  189.0 0.1 fusion.52
  189.1 0.1 broadcast_in_dim.82
  189.2 0.3 copy.46
  189.5 0.1 exp.11
  189.7 0.1 pad.3.clone
  189.8 4.5 %fusion.14 = f32[256,1024]{1,0:T(8,128)} fusion(bf16[1024,2048]{1,0:T(8,128)(2,1)} %param.16, bf16[1,256,2048]{2,1,0:T(8,128)(2,1)S(1)} %copy-done.3), kind=kOutput, calls=%fused_computation.24 | convolution fusion | flops 1073741824 | bytes 6291456 | tf_op jit(solution)/shard_map/dot_general | solution.py:17
  194.3 10.9 %reduce-scatter.3.cloned.1.call-done = bf16[40,2048]{1,0:T(8,128)(2,1)} async-done(((bf16[320,2048]{1,0:T(8,128)(2,1)}), bf16[40,2048]{1,0:T(8,128)(2,1)}) %reduce-scatter.3.cloned.1.call-update) | async-done | bytes 163856 | tf_op jit(solution)/shard_map/reduce_scatter | solution.py:150
  205.3 10.9 %all_gather.34 = bf16[160,2048]{1,0:T(8,128)(2,1)S(1)} all-gather(bf16[40,2048]{1,0:T(8,128)(2,1)} %reduce-scatter.3.cloned.1.call-done), channel_id=1, replica_groups=mesh['expert'=4,'seq'=8] {'expert'}, dimensions={0}, use_global_device_ids=true | all-gather | bytes 819200 | tf_op jit(solution)/shard_map/all_gather | solution.py:151
  216.1 0.5 fusion.29
  216.6 22.9 %reduce-scatter.5.cloned.1.call-done = bf16[40,2048]{1,0:T(8,128)(2,1)} async-done(((bf16[320,2048]{1,0:T(8,128)(2,1)}), bf16[40,2048]{1,0:T(8,128)(2,1)}) %reduce-scatter.5.cloned.1.call-update) | async-done | bytes 163856 | tf_op jit(solution)/shard_map/reduce_scatter | solution.py:150
  239.5 11.4 %all_gather.37 = bf16[160,2048]{1,0:T(8,128)(2,1)S(1)} all-gather(bf16[40,2048]{1,0:T(8,128)(2,1)} %reduce-scatter.5.cloned.1.call-done), channel_id=1, replica_groups=mesh['expert'=4,'seq'=8] {'expert'}, dimensions={0}, use_global_device_ids=true | all-gather | bytes 819200 | tf_op jit(solution)/shard_map/all_gather | solution.py:151
  250.9 0.5 fusion
  251.5 2.9 fusion.55
  254.4 0.3 fusion.11
  254.7 0.8 maximum_maximum_fusion
  255.6 0.2 slice_reduce_fusion.1
  255.8 0.1 broadcast_in_dim.80
  255.8 0.1 broadcast_in_dim.81
  256.0 0.2 convolution_select_fusion
  256.1 6.7 %weight_grads.6.refs_2_ = f32[2,1024,2048]{2,1,0:T(8,128)} custom-call(bf16[320,1024]{1,0:T(8,128)(2,1)} %get-tuple-element.28.refs_0_, bf16[320,2048]{1,0:T(8,128)(2,1)} %all-gather.14.cloned.1.call-done.dy_ref.refs_1_), custom_call_target="tpu_custom_call" | custom-call | flops 1342177280 | bytes 8388608 | tf_op jit(solution)/shard_map/weight_grads/pallas_call | solution.py:87
  262.8 6.6 %weight_grads.7 = f32[2,1024,2048]{2,1,0:T(8,128)} custom-call(bf16[320,1024]{1,0:T(8,128)(2,1)} %get-tuple-element.27.refs_0_, bf16[320,2048]{1,0:T(8,128)(2,1)} %all-gather.18.cloned.1.call-done.dy_ref.refs_1_, f32[2,1024,2048]{2,1,0:T(8,128)} %weight_grads.6.refs_2_), custom_call_target="tpu_custom_call", output_to_operand_aliasing={{}: (2, {})} | custom-call | flops 1342177280 | bytes 8388608 | tf_op jit(solution)/shard_map/weight_grads/pallas_call | solution.py:87
  269.4 9.8 %weight_grads.4 = (f32[2,2048,1024]{2,1,0:T(8,128)}, f32[2,2048,1024]{2,1,0:T(8,128)}) custom-call(bf16[320,2048]{1,0:T(8,128)(2,1)} %all-gather.12.cloned.1.call-done.x_ref.refs_0_, bf16[320,1024]{1,0:T(8,128)(2,1)} %get-tuple-element.21.refs_1_, bf16[320,1024]{1,0:T(8,128)(2,1)} %get-tuple-element.22.refs_2_), custom_call_target="tpu_custom_call" | custom-call | flops 2684354560 | bytes 16777216 | tf_op jit(solution)/shard_map/weight_grads/pallas_call | solution.py:87
  279.2 9.8 %weight_grads.5 = (f32[2,2048,1024]{2,1,0:T(8,128)}, f32[2,2048,1024]{2,1,0:T(8,128)}) custom-call(bf16[320,2048]{1,0:T(8,128)(2,1)} %all-gather.16.cloned.1.call-done.x_ref.refs_0_, bf16[320,1024]{1,0:T(8,128)(2,1)} %get-tuple-element.19.refs_1_, bf16[320,1024]{1,0:T(8,128)(2,1)} %get-tuple-element.20.refs_2_, ...), custom_call_target="tpu_custom_call", output_to_operand_aliasing={{0}: (3, {}), {1}: (4, {})} | custom-call | flops 2684354560 | bytes 16777216 | tf_op jit(solution)/shard_map/weight_grads/pallas_call | solution.py:87
  289.0 0.2 copy.43
  289.2 2.1 fusion.1
  291.3 1.7 fusion.19
  293.0 0.9 fusion.42
  294.0 2.6 fusion.10
  296.6 1.0 copy.47
  (38 shorter events, 0.3 us)
Async XLA Ops:
  7.2 248.8 %copy-start = (bf16[1,256,128]{2,1,0:T(8,128)(2,1)S(1)}, bf16[1,256,128]{2,1,0:T(8,128)(2,1)}, u32[]{:S(2)}) copy-start(bf16[1,256,128]{2,1,0:T(8,128)(2,1)} %param.17) | copy-start | bytes 196612
  7.2 33.2 %all-gather.10.cloned.1.call-start = ((), (), s32[]{:S(2)}) async-start(), calls=%async_computation.2 | async-start | bytes 1392640 | tf_op jit(solution)/shard_map/all_gather | solution.py:121
  9.7 59.2 %all-gather.20.cloned.1.call-start = ((), (), s32[]{:S(2)}) async-start(), calls=%async_computation.9 | async-start | bytes 1310720 | tf_op jit(solution)/shard_map/all_gather | solution.py:122
  10.4 84.1 %all-gather.12.cloned.1.call-start = ((), (), s32[]{:S(2)}) async-start(), calls=%async_computation.3 | async-start | bytes 1474560 | tf_op jit(solution)/shard_map/all_gather | solution.py:142
  43.7 75.8 %all-gather.14.cloned.1.call-start = ((), (), s32[]{:S(2)}) async-start(), calls=%async_computation.4 | async-start | bytes 1474560 | tf_op jit(solution)/shard_map/all_gather | solution.py:142
  71.0 73.5 %all-gather.16.cloned.1.call-start = ((), (), s32[]{:S(2)}) async-start(), calls=%async_computation.6 | async-start | bytes 1474560 | tf_op jit(solution)/shard_map/all_gather | solution.py:142
  73.3 96.3 %all-gather.18.cloned.1.call-start = ((), (), s32[]{:S(2)}) async-start(), calls=%async_computation.7 | async-start | bytes 1474560 | tf_op jit(solution)/shard_map/all_gather | solution.py:142
  75.6 129.7 %reduce-scatter.3.cloned.1.call-start = ((), (), s32[]{:S(2)}) async-start(), calls=%async_computation.5 | async-start | bytes 1474560 | tf_op jit(solution)/shard_map/reduce_scatter | solution.py:150
  138.2 50.0 %copy-start.7 = (f32[1,16,256]{2,1,0:T(8,128)S(1)}, f32[1,16,256]{2,1,0:T(8,128)}, u32[]{:S(2)}) copy-start(f32[1,16,256]{2,1,0:T(8,128)} %param.19) | copy-start | bytes 49156
  138.2 101.4 %reduce-scatter.5.cloned.1.call-start = ((), (), s32[]{:S(2)}) async-start(), calls=%async_computation.8 | async-start | bytes 1474560 | tf_op jit(solution)/shard_map/reduce_scatter | solution.py:150
  188.1 1.7 copy-start.3
  188.1 104.9 %all-gather.22.cloned.1.call-start = ((), (), s32[]{:S(2)}) async-start(), calls=%async_computation.10 | async-start | bytes 2654208 | tf_op jit(solution)/shard_map/all_gather | solution.py:180
  189.2 5.1 %copy-start.1 = (f32[256,16,64]{0,2,1:T(8,128)}, f32[256,16,64]{0,2,1:T(8,128)S(1)}, u32[]{:S(2)}) copy-start(f32[256,16,64]{0,2,1:T(8,128)S(1)} %broadcast_in_dim.82) | copy-start | bytes 3145732
  239.5 11.9 %copy-start.8 = (bf16[1024,2048]{1,0:T(8,128)(2,1)S(1)}, bf16[1024,2048]{1,0:T(8,128)(2,1)}, u32[]{:S(2)}) copy-start(bf16[1024,2048]{1,0:T(8,128)(2,1)} %param.16) | copy-start | bytes 12582916
  251.4 3.3 %copy-start.4 = (bf16[256,2048]{1,0:T(8,128)(2,1)}, bf16[256,2048]{1,0:T(8,128)(2,1)S(1)}, u32[]{:S(2)}) copy-start(bf16[256,2048]{1,0:T(8,128)(2,1)S(1)} %fusion) | copy-start | bytes 3145732
  251.4 2.9 copy-start.6
  289.0 2.3 copy-start.5
  289.0 5.0 %copy-start.2 = (f32[256,16,64]{0,2,1:T(8,128)S(1)}, f32[256,16,64]{0,2,1:T(8,128)}, u32[]{:S(2)}) copy-start(f32[256,16,64]{0,2,1:T(8,128)} %copy-done.1) | copy-start | bytes 3145732
Sparse Core Ops, SparseCore 0:
  10.4 29.8 all-gather.9
  42.2 26.6 all-gather.19
  71.1 23.4 all-gather.11
  96.6 22.9 all-gather.13
  121.6 22.9 all-gather.15
  146.7 22.9 all-gather.17
  172.5 32.7 reduce-scatter.2
  208.1 31.3 reduce-scatter.4
  255.7 29.5 all-gather.21
where the time goes:
time: 305 us; the launch traced here: 304 us
  waiting for transfers between devices  165 us (54%)
  Pallas kernels  69.9 us (23%)
  matrix products  22.3 us (7%)
  blocking collectives  22.3 us (7%)
  between operations  14.1 us (5%)
  other arithmetic  6.86 us (2%)
  local copies, waits for them, and re-layouts  3.41 us (1%)
    all_gather x4, waiting for transfers between devices, body(): lax.all_gather(part, 'seq', axis=0, tiled=True)  75.4 us
    pallas_call x2, Pallas kernels, expert_terms(): pl.pallas_call(terms_kernel, grid=(hidden // tile,), in_specs=[whole, who...  37 us
    reduce_scatter x2, waiting for transfers between devices, body(): summed = lax.psum_scatter(back, 'seq', scatter_dimension=0, tiled=True)  33.8 us
    pallas_call x4, Pallas kernels, weight_grads(): pl.pallas_call(kernel, grid=(width // tile,), in_specs=[pl.BlockSpec((row...  32.8 us
    all_gather x1, waiting for transfers between devices, body(): x_all = lax.all_gather(labelled, 'expert', axis=0, tiled=True)  29.9 us
    all_gather x1, waiting for transfers between devices, body(): dy_all = lax.all_gather(out_grad[0], 'expert', axis=0, tiled=True)  25 us
    all_gather x2, blocking collectives, body(): returned.append(lax.all_gather(summed, 'expert', axis=0, tiled=True))  22.3 us
    dot_general x11, matrix products, mm(): return lax.dot_general(a, b, dims, preferred_element_type=jnp.float32)  20.2 us
  transfers between devices with their start and end apart: 9, of which 8 were waited for; matrix products, arithmetic and copies ran while one was open for 7% of the time, Pallas kernels for 23%

commit v1 on v0

v1 whole, which is shorter than its diff:
```python
import jax
import jax.numpy as jnp
from jax import lax
from jax.experimental import pallas as pl
from jax.experimental.pallas import tpu as pltpu
from jax.sharding import PartitionSpec as P

P_SIZE = 64
CAP = 10
VMEM = 60 * 1024 * 1024
NN = (((1,), (0,)), ((), ()))
NT = (((1,), (1,)), ((), ()))
TN = (((0,), (0,)), ((), ()))


def mm(a, b, dims):
    return lax.dot_general(a, b, dims, preferred_element_type=jnp.float32)


def terms_kernel(x_ref, dy_ref, wg_ref, wu_ref, wd_ref, h_ref, g_ref, u_ref, back_ref, acc):
    step = pl.program_id(0)
    x = x_ref[0]
    gate = mm(x, wg_ref[0], NN)
    up = mm(x, wu_ref[0], NN)
    grad = mm(dy_ref[0], wd_ref[0], NT)
    logistic = jax.nn.sigmoid(gate)
    activated = gate * logistic
    h_ref[...] = (activated * up).astype(jnp.bfloat16)
    up_term = (grad * activated).astype(jnp.bfloat16)
    gate_term = (grad * up * logistic * (1.0 + gate * (1.0 - logistic))).astype(jnp.bfloat16)
    g_ref[...] = gate_term
    u_ref[...] = up_term
    part = mm(gate_term, wg_ref[0], NT) + mm(up_term, wu_ref[0], NT)

    @pl.when(step == 0)
    def _():
        acc[...] = part

    @pl.when(step > 0)
    def _():
        acc[...] += part

    @pl.when(step == pl.num_programs(0) - 1)
    def _():
        back_ref[...] = acc[...].astype(jnp.bfloat16)


def expert_terms(e, local, gathered, w_gate, w_up, w_down):
    rows, width = gathered.shape[1:]
    hidden = w_gate.shape[2]
    tile = min(512, hidden)
    whole = pl.BlockSpec((rows, width), lambda i: (0, 0))
    part = pl.BlockSpec((rows, tile), lambda i: (0, i))
    column = pl.BlockSpec((1, width, tile), lambda i: (e, 0, i))
    row = pl.BlockSpec((1, tile, width), lambda i: (e, i, 0))
    term = jax.ShapeDtypeStruct((rows, hidden), jnp.bfloat16)
    return pl.pallas_call(
        terms_kernel,
        grid=(hidden // tile,),
        in_specs=[
            pl.BlockSpec((1, rows, width), lambda i: (e, 0, 0)),
            pl.BlockSpec((1, rows, width), lambda i: (local + e, 0, 0)),
            column,
            column,
            row,
        ],
        out_specs=[part, part, part, whole],
        out_shape=[term, term, term, jax.ShapeDtypeStruct((rows, width), jnp.bfloat16)],
        scratch_shapes=[pltpu.VMEM((rows, width), jnp.float32)],
        compiler_params=pltpu.CompilerParams(vmem_limit_bytes=VMEM),
        cost_estimate=pl.CostEstimate(
            flops=10 * rows * width * hidden,
            bytes_accessed=6 * width * hidden + 6 * rows * width,
            transcendentals=rows * hidden,
        ),
        name="expert_terms",
    )(gathered, gathered, w_gate, w_up, w_down)


def weight_grads(e, count, left, rights, held):
    left, left_at = left
    rows, width = left.shape[1:]
    breadth = rights[0][0].shape[2]
    tile = min(256, width)
    number = len(rights)

    def kernel(*refs):
        left_ref, right_refs, out_refs = refs[0], refs[1 : 1 + number], refs[-number:]
        for right_ref, out_ref in zip(right_refs, out_refs):
            out_ref[0] = mm(left_ref[0], right_ref[0], TN)

    out = pl.BlockSpec((1, tile, breadth), lambda i: (e, i, 0))
    kept = [] if held is None else list(held)
    return pl.pallas_call(
        kernel,
        grid=(width // tile,),
        in_specs=[pl.BlockSpec((1, rows, tile), lambda i: (left_at, 0, i))]
        + [pl.BlockSpec((1, rows, breadth), lambda i, at=at: (at, 0, 0)) for _, at in rights]
        + [pl.BlockSpec(memory_space=pl.ANY)] * len(kept),
        out_specs=[out] * number,
        out_shape=[jax.ShapeDtypeStruct((count, width, breadth), jnp.float32)] * number,
        input_output_aliases={1 + number + k: k for k in range(len(kept))},
        compiler_params=pltpu.CompilerParams(vmem_limit_bytes=VMEM),
        cost_estimate=pl.CostEstimate(
            flops=2 * number * rows * width * breadth,
            bytes_accessed=4 * number * width * breadth,
            transcendentals=0,
        ),
        name="weight_grads",
    )(left, *[right for right, _ in rights], *kept)


def body(moe_input, out_grad, expert_id, w_gate, w_up, w_down, w_out, b_proj, c_proj, log_decay):
    groups = lax.axis_size("expert")
    group = lax.axis_index("expert")
    shards = lax.axis_size("seq")
    shard = lax.axis_index("seq")
    local = w_gate.shape[0]
    tokens, width = moe_input.shape[1:]
    heads = w_out.shape[0] // P_SIZE
    lanes = heads * P_SIZE
    length, state = b_proj.shape[1:]
    bf = jnp.bfloat16

    def places(labels):
        here = jnp.arange(labels.shape[0], dtype=jnp.int32)
        same = (
            (labels[:, None] == labels[None, :])
            & (here[:, None] // tokens == here[None, :] // tokens)
            & (here[None, :] < here[:, None])
        )
        return (here // tokens) * CAP + jnp.sum(same.astype(jnp.int32), axis=1)

    span = groups * CAP
    kinds = 2 * local
    block = kinds * CAP
    labels = expert_id[0, :, 0]
    sent_row = (labels // local) * block + (labels % local) * CAP + places(labels)
    sent_rows = jnp.concatenate([sent_row, sent_row + local * CAP])
    placing = (
        jnp.arange(groups * block, dtype=jnp.int32)[:, None] == sent_rows[None, :]
    ).astype(bf)
    both = jnp.concatenate([moe_input[0], out_grad[0]], axis=0)
    picked = mm(placing, both, NN).astype(bf)
    received = lax.all_to_all(
        picked.reshape(groups, block, width), "expert", split_axis=0, concat_axis=0, tiled=True
    ).reshape(groups * block, width)
    rank = jnp.arange(groups * block, dtype=jnp.int32)
    source = (rank % span) // CAP * block + rank // span * CAP + rank % CAP
    order = (source[:, None] == rank[None, :]).astype(bf)
    arranged = mm(order, received, NN).astype(bf).reshape(kinds, span, width)
    gathered = lax.all_gather(arranged, "seq", axis=1, tiled=True)

    late = jnp.concatenate(
        [out_grad[0], jnp.broadcast_to(expert_id[0], (tokens, 128)).astype(bf)], axis=1
    )
    gathered, late = lax.optimization_barrier((gathered, late))
    dy_all = lax.all_gather(late, "expert", axis=0, tiled=True)

    terms = [expert_terms(e, local, gathered, w_gate, w_up, w_down) for e in range(local)]
    back = jnp.stack([t[3].reshape(shards, span, width) for t in terms], axis=1)
    summed = lax.psum_scatter(
        back.reshape(shards, local * span, width), "seq", scatter_dimension=0, tiled=True
    )[0]
    gate_up, down = None, None
    for e in range(local):
        hidden, gate_term, up_term, _ = terms[e]
        gate_up = weight_grads(
            e, local, (gathered, e), [(gate_term[None], 0), (up_term[None], 0)], gate_up
        )
        down = weight_grads(e, local, (hidden[None], 0), [(gathered, local + e)], down)

    here = jnp.arange(length, dtype=jnp.int32)
    labels = dy_all[:, width].astype(jnp.int32)
    place = places(labels)
    acum = jnp.cumsum(log_decay[0], axis=1)
    b_rows, c_rows = b_proj[0], c_proj[0]
    wide = jnp.repeat(acum.T, P_SIZE, axis=1)
    grow = jnp.exp(wide)
    tail = jnp.exp(wide[-1:] - wide)
    total = grow[-1:]
    high = total.astype(bf)
    low = (total - high.astype(jnp.float32)).astype(bf)
    later = here[:, None] >= here[None, :]
    scores = jnp.where(later, mm(c_rows, b_rows, NT), 0.0)
    difference = jnp.where(later[None], acum[:, :, None] - acum[:, None, :], 0.0)
    weight = (jnp.exp(difference) * scores[None]).astype(bf)
    head_base = mm(dy_all[:, :width], w_out, NT)
    summed, gate_up, down, head_base, weight, grow, tail = lax.optimization_barrier(
        (summed, gate_up, down, head_base, weight, grow, tail)
    )
    returned = lax.all_gather(summed, "expert", axis=0, tiled=True)
    row = (labels // local) * (local * span) + (labels % local) * span + place
    take = (row[:, None] == jnp.arange(groups * local * span, dtype=jnp.int32)[None, :]).astype(bf)
    expert_all = mm(take, returned, NN)
    expert_all = expert_all.astype(bf)
    own = lax.dynamic_slice_in_dim(expert_all, group * tokens, tokens, axis=0)
    input_grad = (out_grad[0].astype(jnp.float32) + own.astype(jnp.float32)).astype(bf)

    head_out = head_base + mm(expert_all, w_out, NT)
    summary = mm(c_rows, (grow * head_out).astype(bf), TN).astype(bf)
    sent = jnp.concatenate([summary, high, low, jnp.zeros((14, lanes), bf)], axis=0)
    states = lax.all_to_all(sent, "seq", split_axis=1, concat_axis=0, tiled=True)
    states = states.reshape(shards, state + 16, lanes // shards).astype(jnp.float32)
    local_part = jnp.einsum(
        "hts,thp->shp",
        weight,
        head_out.astype(bf).reshape(length, heads, P_SIZE),
        preferred_element_type=jnp.float32,
    ).reshape(length, lanes)
    carry = jnp.zeros((state, lanes // shards), jnp.float32)
    carries = [carry]
    for r in range(shards - 1, 0, -1):
        whole = states[r, state : state + 1] + states[r, state + 1 : state + 2]
        carry = states[r, :state] + whole * carry
        carries.append(carry)
    carries = jnp.concatenate(carries[::-1], axis=0).astype(bf)
    carried = lax.all_to_all(carries, "seq", split_axis=0, concat_axis=1, tiled=True)
    cross = tail * mm(b_rows, carried, NN)
    head_grad = (local_part + cross).astype(bf)
    return (head_grad[None], input_grad[None], gate_up[0], gate_up[1], down[0])


def solution(mesh):
    return jax.shard_map(
        body,
        mesh=mesh,
        in_specs=(
            P("seq", "expert", None),
            P("seq", "expert", None),
            P("seq", "expert", None),
            P("expert", None, "seq"),
            P("expert", None, "seq"),
            P("expert", "seq", None),
            P("expert", None),
            P("seq", None, None),
            P("seq", None, None),
            P("seq", "expert", None),
        ),
        out_specs=(
            P("seq", None, "expert"),
            P("seq", "expert", None),
            P("expert", None, "seq"),
            P("expert", None, "seq"),
            P("expert", "seq", None),
        ),
        check_vma=False,
    )
```

time: 305 us -> 238 us (0.78)
  waiting for transfers between devices: 165 us -> 104 us
  blocking collectives: 22.3 us -> 0 us
  starting transfers between devices: 0.37 us -> 13.5 us
  other arithmetic: 6.86 us -> 18.1 us
  Pallas kernels: 69.9 us -> 60.3 us
  local copies, waits for them, and re-layouts: 3.41 us -> 8.14 us
  matrix products: 22.3 us -> 18.7 us
    all_gather x7 -> x3, waiting for transfers between devices: 130 us -> 79.9 us  [the longest x1 55.6 us: body(): gathered = lax.all_gather(arranged, 'seq', axis=1, tiled=True)]
    reduce_scatter x2 -> x1, waiting for transfers between devices: 33.8 us -> 0.01 us  [body(): lax.psum_scatter(back.reshape(shards, local * span, width), 'seq', scatte...]
    all_to_all x0 -> x3, waiting for transfers between devices: none -> 24.3 us  [the longest x1 9.4 us: body(): lax.all_to_all(picked.reshape(groups, block, width), 'expert', split_axis...]
    all_gather x2 -> x0, blocking collectives: 22.3 us -> none  [body(): returned.append(lax.all_gather(summed, 'expert', axis=0, tiled=True))]
    all_to_all x0 -> x3, starting transfers between devices: none -> 13.2 us  [the longest x1 5.16 us: body(): lax.all_to_all(picked.reshape(groups, block, width), 'expert', split_axis...]
    pallas_call x6, Pallas kernels: 69.9 us -> 60.3 us  [the longest x4 32.9 us: weight_grads(): pl.pallas_call(kernel, grid=(width // tile,), in_specs=[pl.BlockSpec((1,...]
    unnamed x0 -> x7, other arithmetic: none -> 4.39 us
    dot_general x11 -> x8, matrix products: 20.2 us -> 17.2 us  [mm(): return lax.dot_general(a, b, dims, preferred_element_type=jnp.float32)]
  transfers between devices with their start and end apart: 9 -> 7, of which waited for: 8 -> 5; matrix products, arithmetic and copies ran while one was open for 7% -> 10% of each run, Pallas kernels for 23% -> 25%
where the time goes in v1:
time: 238 us; the launch traced here: 237 us
  waiting for transfers between devices  104 us (44%)
  Pallas kernels  60.3 us (25%)
  matrix products  18.7 us (8%)
  other arithmetic  18.1 us (8%)
  between operations  14 us (6%)
  starting transfers between devices  13.5 us (6%)
  local copies, waits for them, and re-layouts  8.14 us (3%)
    all_gather x1, waiting for transfers between devices, body(): gathered = lax.all_gather(arranged, 'seq', axis=1, tiled=True)  55.6 us
    pallas_call x4, Pallas kernels, weight_grads(): pl.pallas_call(kernel, grid=(width // tile,), in_specs=[pl.BlockSpec((1,...  32.9 us
    pallas_call x2, Pallas kernels, expert_terms(): pl.pallas_call(terms_kernel, grid=(hidden // tile,), in_specs=[pl.BlockSp...  27.4 us
    all_gather x1, waiting for transfers between devices, body(): returned = lax.all_gather(summed, 'expert', axis=0, tiled=True)  24.4 us
    dot_general x8, matrix products, mm(): return lax.dot_general(a, b, dims, preferred_element_type=jnp.float32)  17.2 us
    all_to_all x1, waiting for transfers between devices, body(): lax.all_to_all(picked.reshape(groups, block, width), 'expert', split_axis...  9.4 us
    all_to_all x1, waiting for transfers between devices, body(): lax.all_to_all(carries, 'seq', split_axis=0, concat_axis=1, tiled=True)  7.94 us
    all_to_all x1, waiting for transfers between devices, body(): lax.all_to_all(sent, 'seq', split_axis=1, concat_axis=0, tiled=True)  6.95 us
  transfers between devices with their start and end apart: 7, of which 5 were waited for; matrix products, arithmetic and copies ran while one was open for 10% of the time, Pallas kernels for 25%

profile of v1, /device:TPU:0, one launch (start us, length us, event | category | flops | bytes accessed | tf_op | source)
XLA Modules:
  0.0 237.0 jit_solution(11564996901777492084)
XLA Ops:
  7.2 1.0 convert_reduce_fusion.1
  8.2 0.7 broadcast_add_fusion
  8.9 0.1 pad_add_fusion
  8.9 2.2 convolution_convert_fusion.2
  11.1 5.2 %all-to-all-start = ((bf16[4,40,2048]{2,1,0:T(8,128)(2,1)}), bf16[4,40,2048]{2,1,0:T(8,128)(2,1)S(1)}, u32[]{:S(2)}, u32[]{:S(2)}) async-start(bf16[4,40,2048]{2,1,0:T(8,128)(2,1)} %bitcast.3), calls=%async_computation | async-start | bytes 1310720 | tf_op jit(solution)/shard_map/all_to_all | solution.py:145
  16.3 9.4 %all-to-all-done = bf16[4,40,2048]{2,1,0:T(8,128)(2,1)S(1)} async-done(((bf16[4,40,2048]{2,1,0:T(8,128)(2,1)}), bf16[4,40,2048]{2,1,0:T(8,128)(2,1)S(1)}, u32[]{:S(2)}, u32[]{:S(2)}) %all-to-all-start) | async-done | bytes 655392 | tf_op jit(solution)/shard_map/all_to_all | solution.py:145
  25.7 1.2 convolution_convert_fusion.1
  27.0 0.0 all-gather.6.cloned.1.call-start
  27.0 0.1 broadcast_in_dim.82
  27.1 0.7 pad_maximum_fusion.1
  27.8 55.6 %all-gather.4.cloned.1.call-done.x_ref.dy_ref.refs_0_.refs_1_ = bf16[4,320,2048]{2,1,0:T(8,128)(2,1)} async-done(((bf16[4,40,2048]{2,1,0:T(8,128)(2,1)}), bf16[4,320,2048]{2,1,0:T(8,128)(2,1)}) %all-gather.4.cloned.1.call-update) | async-done | bytes 5242896 | tf_op jit(solution)/shard_map/all_gather | solution.py:152
  83.4 0.0 all-gather.6.cloned.1.call-update
  83.4 0.0 reduce-scatter.2.cloned.1.call-start
  83.5 13.7 %expert_terms.3 = (bf16[320,1024]{1,0:T(8,128)(2,1)}, bf16[320,1024]{1,0:T(8,128)(2,1)}, bf16[320,1024]{1,0:T(8,128)(2,1)}, bf16[320,2048]{1,0:T(8,128)(2,1)}) custom-call(bf16[4,320,2048]{2,1,0:T(8,128)(2,1)} %all-gather.4.cloned.1.call-done.x_ref.dy_ref.refs_0_.refs_1_, bf16[4,320,2048]{2,1,0:T(8,128)(2,1)} %all-gather.4.cloned.1.call-done.x_ref.dy_ref.refs_0_.refs_1_, ...), custom_call_target="tpu_custom_call" | custom-call | flops 6710886400 | bytes 16515072 | tf_op jit(solution)/shard_map/expert_terms/pallas_call | solution.py:57
  97.2 13.7 %expert_terms.2 = (bf16[320,1024]{1,0:T(8,128)(2,1)}, bf16[320,1024]{1,0:T(8,128)(2,1)}, bf16[320,1024]{1,0:T(8,128)(2,1)}, bf16[320,2048]{1,0:T(8,128)(2,1)}) custom-call(bf16[4,320,2048]{2,1,0:T(8,128)(2,1)} %all-gather.4.cloned.1.call-done.x_ref.dy_ref.refs_0_.refs_1_, bf16[4,320,2048]{2,1,0:T(8,128)(2,1)} %all-gather.4.cloned.1.call-done.x_ref.dy_ref.refs_0_.refs_1_, ...), custom_call_target="tpu_custom_call" | custom-call | flops 6710886400 | bytes 16515072 | tf_op jit(solution)/shard_map/expert_terms/pallas_call | solution.py:57
  110.9 3.0 %pad_maximum_fusion = bf16[8,2,40,2048]{3,2,1,0:T(8,128)(2,1)} fusion(bf16[8,1,40,2048]{3,2,1,0:T(8,128)(2,1)S(1)} %bitcast.167, bf16[8,1,40,2048]{3,2,1,0:T(8,128)(2,1)} %bitcast.168), kind=kLoop, calls=%fused_computation.1 | loop fusion | flops 1310720 | bytes 5242880 | tf_op jit(solution)/shard_map/stack | solution.py:161
  113.9 0.0 reduce-scatter.2.cloned.1.call-update
  114.0 0.2 all-gather.8.cloned.1.call-start
  114.2 0.6 reduce-window.6
  114.8 0.2 slice_reduce_fusion
  115.0 0.7 fusion.53
  115.7 0.1 broadcast_in_dim.92
  115.8 0.3 copy.71
  116.1 0.1 exp.10
  116.3 0.2 slice_reduce_fusion.1
  116.5 0.1 broadcast_in_dim.93
  116.5 0.1 broadcast_in_dim.94
  116.6 1.2 subtract_exponential_fusion
  117.9 0.2 convolution_select_fusion
  118.0 1.8 multiply_convert_fusion
  119.8 6.7 %weight_grads.6.refs_2_ = f32[2,1024,2048]{2,1,0:T(8,128)} custom-call(bf16[1,320,1024]{2,1,0:T(8,128)(2,1)} %bitcast.171, bf16[4,320,2048]{2,1,0:T(8,128)(2,1)} %all-gather.4.cloned.1.call-done.x_ref.dy_ref.refs_0_.refs_1_), custom_call_target="tpu_custom_call" | custom-call | flops 1342177280 | bytes 8388608 | tf_op jit(solution)/shard_map/weight_grads/pallas_call | solution.py:94
  126.5 6.7 %weight_grads.7 = f32[2,1024,2048]{2,1,0:T(8,128)} custom-call(bf16[1,320,1024]{2,1,0:T(8,128)(2,1)} %bitcast.174, bf16[4,320,2048]{2,1,0:T(8,128)(2,1)} %all-gather.4.cloned.1.call-done.x_ref.dy_ref.refs_0_.refs_1_, f32[2,1024,2048]{2,1,0:T(8,128)} %weight_grads.6.refs_2_), custom_call_target="tpu_custom_call", output_to_operand_aliasing={{}: (2, {})} | custom-call | flops 1342177280 | bytes 8388608 | tf_op jit(solution)/shard_map/weight_grads/pallas_call | solution.py:94
  133.1 9.8 %weight_grads.4 = (f32[2,2048,1024]{2,1,0:T(8,128)}, f32[2,2048,1024]{2,1,0:T(8,128)}) custom-call(bf16[4,320,2048]{2,1,0:T(8,128)(2,1)} %all-gather.4.cloned.1.call-done.x_ref.dy_ref.refs_0_.refs_1_, bf16[1,320,1024]{2,1,0:T(8,128)(2,1)} %bitcast.181, bf16[1,320,1024]{2,1,0:T(8,128)(2,1)} %bitcast.182), custom_call_target="tpu_custom_call" | custom-call | flops 2684354560 | bytes 16777216 | tf_op jit(solution)/shard_map/weight_grads/pallas_call | solution.py:94
  143.0 9.8 %weight_grads.5 = (f32[2,2048,1024]{2,1,0:T(8,128)}, f32[2,2048,1024]{2,1,0:T(8,128)}) custom-call(bf16[4,320,2048]{2,1,0:T(8,128)(2,1)} %all-gather.4.cloned.1.call-done.x_ref.dy_ref.refs_0_.refs_1_, bf16[1,320,1024]{2,1,0:T(8,128)(2,1)} %bitcast.172, bf16[1,320,1024]{2,1,0:T(8,128)(2,1)} %bitcast.173, ...), custom_call_target="tpu_custom_call", output_to_operand_aliasing={{0}: (3, {}), {1}: (4, {})} | custom-call | flops 2684354560 | bytes 16777216 | tf_op jit(solution)/shard_map/weight_grads/pallas_call | solution.py:94
  152.8 4.8 %fusion.5 = f32[256,1024]{1,0:T(8,128)} fusion(bf16[1024,2048]{1,0:T(8,128)(2,1)} %param.16, bf16[256,2176]{1,0:T(8,128)(2,1)} %all-gather.6.cloned.1.call-done), kind=kOutput, calls=%fused_computation.14 | convolution fusion | flops 1073741824 | bytes 6291456 | tf_op jit(solution)/shard_map/dot_general | solution.py:17
  157.5 0.0 all-gather.8.cloned.1.call-update
  157.6 0.7 pad.3.clone
  158.3 1.5 slice.116
  159.7 0.9 copy.77
  160.7 0.2 convert_reduce_fusion
  160.9 24.4 %all-gather.8.cloned.1.call-done = bf16[320,2048]{1,0:T(8,128)(2,1)} async-done(((bf16[80,2048]{1,0:T(8,128)(2,1)}), bf16[320,2048]{1,0:T(8,128)(2,1)}) %all-gather.8.cloned.1.call-update) | async-done | bytes 1310736 | tf_op jit(solution)/shard_map/all_gather | solution.py:192
  185.3 2.1 convolution_convert_fusion
  187.4 4.9 %fusion.57 = (bf16[256,1024]{1,0:T(8,128)(2,1)}, f32[256,1024]{1,0:T(8,128)S(1)}) fusion(f32[256,1024]{1,0:T(8,128)} %fusion.5, bf16[256,2048]{1,0:T(8,128)(2,1)S(1)} %convolution_convert_fusion, bf16[1024,2048]{1,0:T(8,128)(2,1)} %param.16), kind=kOutput, calls=%fused_computation.137 | convolution fusion | flops 1074266112 | bytes 7864320 | tf_op jit(solution)/shard_map/dot_general | solution.py:17
  192.3 0.3 fusion.4
  192.6 0.9 copy_bitcast_fusion
  193.5 4.6 %all-to-all-start.1 = ((bf16[144,8,128]{2,0,1:T(8,128)(2,1)}), bf16[144,8,128]{2,0,1:T(8,128)(2,1)}, u32[]{:S(2)}, u32[]{:S(2)}) async-start(bf16[144,8,128]{2,0,1:T(8,128)(2,1)} %copy_bitcast_fusion), calls=%async_computation.2 | async-start | bytes 589824 | tf_op jit(solution)/shard_map/all_to_all | solution.py:203
  198.1 2.1 copy.73
  200.2 1.5 fusion.58
  201.7 6.9 %all-to-all-done.1 = bf16[144,8,128]{2,0,1:T(8,128)(2,1)} async-done(((bf16[144,8,128]{2,0,1:T(8,128)(2,1)}), bf16[144,8,128]{2,0,1:T(8,128)(2,1)}, u32[]{:S(2)}, u32[]{:S(2)}) %all-to-all-start.1) | async-done | bytes 294944 | tf_op jit(solution)/shard_map/all_to_all | solution.py:203
  208.6 1.0 convert_bitcast_fusion
  209.7 0.7 fusion.29
  210.3 0.6 convert_dynamic-update-slice_fusion.4
  210.9 0.6 convert_dynamic-update-slice_fusion.3
  211.6 0.6 convert_dynamic-update-slice_fusion.2
  212.2 0.6 convert_dynamic-update-slice_fusion.1
  212.8 0.6 convert_dynamic-update-slice_fusion
  213.4 0.6 fusion.28
  214.1 0.6 constant_dynamic-update-slice_fusion
  214.7 3.4 %all-to-all-start.2 = ((bf16[8,128,128]{2,1,0:T(8,128)(2,1)}), bf16[8,128,128]{2,1,0:T(8,128)(2,1)S(1)}, u32[]{:S(2)}, u32[]{:S(2)}) async-start(bf16[8,128,128]{2,1,0:T(8,128)(2,1)} %bitcast.44), calls=%async_computation.3 | async-start | bytes 524288 | tf_op jit(solution)/shard_map/all_to_all | solution.py:218
  218.1 1.7 fusion.10
  219.8 7.9 %all-to-all-done.2 = bf16[8,128,128]{2,1,0:T(8,128)(2,1)S(1)} async-done(((bf16[8,128,128]{2,1,0:T(8,128)(2,1)}), bf16[8,128,128]{2,1,0:T(8,128)(2,1)S(1)}, u32[]{:S(2)}, u32[]{:S(2)}) %all-to-all-start.2) | async-done | bytes 262176 | tf_op jit(solution)/shard_map/all_to_all | solution.py:218
  227.8 0.2 copy.75
  227.9 1.5 fusion.3
  229.5 1.0 copy.76
  (35 shorter events, 0.2 us)
Async XLA Ops:
  7.2 110.7 %copy-start = (bf16[1,256,128]{2,1,0:T(8,128)(2,1)S(1)}, bf16[1,256,128]{2,1,0:T(8,128)(2,1)}, u32[]{:S(2)}) copy-start(bf16[1,256,128]{2,1,0:T(8,128)(2,1)} %param.17) | copy-start | bytes 196612
  7.2 19.8 %copy-start.6 = (s32[1,64,1]{1,2,0:T(1,128)S(1)}, s32[1,64,1]{1,2,0:T(1,128)}, u32[]{:S(2)}) copy-start(s32[1,64,1]{1,2,0:T(1,128)} %param.12) | copy-start | bytes 772
  7.2 19.9 %copy-start.1 = (bf16[1,64,2048]{2,1,0:T(8,128)(2,1)S(1)}, bf16[1,64,2048]{2,1,0:T(8,128)(2,1)}, u32[]{:S(2)}) copy-start(bf16[1,64,2048]{2,1,0:T(8,128)(2,1)} %param.11) | copy-start | bytes 786436
  11.1 14.6 %all-to-all-start = ((bf16[4,40,2048]{2,1,0:T(8,128)(2,1)}), bf16[4,40,2048]{2,1,0:T(8,128)(2,1)S(1)}, u32[]{:S(2)}, u32[]{:S(2)}) async-start(bf16[4,40,2048]{2,1,0:T(8,128)(2,1)} %bitcast.3), calls=%async_computation | async-start | bytes 1310720 | tf_op jit(solution)/shard_map/all_to_all | solution.py:145
  16.3 67.1 %all-gather.4.cloned.1.call-start = ((), (), s32[]{:S(2)}) async-start(), calls=%async_computation.4 | async-start | bytes 5898240 | tf_op jit(solution)/shard_map/all_gather | solution.py:152
  27.0 125.8 %all-gather.6.cloned.1.call-start = ((), (), s32[]{:S(2)}) async-start(), calls=%async_computation.6 | async-start | bytes 1392640 | tf_op jit(solution)/shard_map/all_gather | solution.py:158
  83.4 74.1 %reduce-scatter.2.cloned.1.call-start = ((), (), s32[]{:S(2)}) async-start(), calls=%async_computation.5 | async-start | bytes 2949120 | tf_op jit(solution)/shard_map/reduce_scatter | solution.py:162
  97.1 13.8 %copy-start.3 = (bf16[320,2048]{1,0:T(8,128)(2,1)S(1)}, bf16[320,2048]{1,0:T(8,128)(2,1)}, u32[]{:S(2)}) copy-start(bf16[320,2048]{1,0:T(8,128)(2,1)} %get-tuple-element.29) | copy-start | bytes 3932164
  110.9 3.3 %copy-start.5 = (f32[1,16,256]{2,1,0:T(8,128)S(1)}, f32[1,16,256]{2,1,0:T(8,128)}, u32[]{:S(2)}) copy-start(f32[1,16,256]{2,1,0:T(8,128)} %param.19) | copy-start | bytes 49156
  113.9 3.9 %copy-start.4 = (bf16[1,256,128]{2,1,0:T(8,128)(2,1)S(1)}, bf16[1,256,128]{2,1,0:T(8,128)(2,1)}, u32[]{:S(2)}) copy-start(bf16[1,256,128]{2,1,0:T(8,128)(2,1)} %param.18) | copy-start | bytes 196612
  114.0 71.3 %all-gather.8.cloned.1.call-start = ((), (), s32[]{:S(2)}) async-start(), calls=%async_computation.7 | async-start | bytes 1638400 | tf_op jit(solution)/shard_map/all_gather | solution.py:192
  187.4 5.2 %copy-start.2 = (bf16[256,2048]{1,0:T(8,128)(2,1)}, bf16[256,2048]{1,0:T(8,128)(2,1)S(1)}, u32[]{:S(2)}) copy-start(bf16[256,2048]{1,0:T(8,128)(2,1)S(1)} %convolution_convert_fusion) | copy-start | bytes 3145732
  187.4 5.2 %copy-start.7 = (bf16[144]{0:T(256)(128)(2,1)S(1)}, bf16[144]{0:T(256)(128)(2,1)}, u32[]{:S(2)}) copy-start(bf16[144]{0:T(256)(128)(2,1)} %pad.3.clone) | copy-start | bytes 868
  193.5 15.2 %all-to-all-start.1 = ((bf16[144,8,128]{2,0,1:T(8,128)(2,1)}), bf16[144,8,128]{2,0,1:T(8,128)(2,1)}, u32[]{:S(2)}, u32[]{:S(2)}) async-start(bf16[144,8,128]{2,0,1:T(8,128)(2,1)} %copy_bitcast_fusion), calls=%async_computation.2 | async-start | bytes 589824 | tf_op jit(solution)/shard_map/all_to_all | solution.py:203
  214.7 13.1 %all-to-all-start.2 = ((bf16[8,128,128]{2,1,0:T(8,128)(2,1)}), bf16[8,128,128]{2,1,0:T(8,128)(2,1)S(1)}, u32[]{:S(2)}, u32[]{:S(2)}) async-start(bf16[8,128,128]{2,1,0:T(8,128)(2,1)} %bitcast.44), calls=%async_computation.3 | async-start | bytes 524288 | tf_op jit(solution)/shard_map/all_to_all | solution.py:218
Sparse Core Ops, SparseCore 0:
  27.1 56.2 all-gather.3
  85.8 25.9 all-gather.5
  114.2 37.4 reduce-scatter.1
  157.7 27.5 all-gather.7

commit v2 on v1

--- a/solution.py
+++ b/solution.py
@@ -189,8 +189,16 @@
     summed, gate_up, down, head_base, weight, grow, tail = lax.optimization_barrier(
         (summed, gate_up, down, head_base, weight, grow, tail)
     )
-    returned = lax.all_gather(summed, "expert", axis=0, tiled=True)
-    row = (labels // local) * (local * span) + (labels % local) * span + place
+    returned = jnp.concatenate(
+        [summed]
+        + [
+            lax.ppermute(summed, "expert", [(i, (i + k) % groups) for i in range(groups)])
+            for k in range(1, groups)
+        ],
+        axis=0,
+    )
+    behind = (group - labels // local + groups) % groups
+    row = behind * (local * span) + (labels % local) * span + place
     take = (row[:, None] == jnp.arange(groups * local * span, dtype=jnp.int32)[None, :]).astype(bf)
     expert_all = mm(take, returned, NN)
     expert_all = expert_all.astype(bf)

time: 238 us -> 229 us (0.962)
  waiting for transfers between devices: 104 us -> 95.3 us
  matrix products: 18.7 us -> 14.6 us
  starting transfers between devices: 13.5 us -> 16.3 us
    all_gather x1 -> x0, waiting for transfers between devices: 24.4 us -> none  [body(): returned = lax.all_gather(summed, 'expert', axis=0, tiled=True)]
    ppermute x0 -> x3, waiting for transfers between devices: none -> 15.5 us  [body(): lax.ppermute(summed, 'expert', [(i, (i + k) % groups) for i in range(grou...]
    dot_general x8, matrix products: 17.2 us -> 13 us  [mm(): return lax.dot_general(a, b, dims, preferred_element_type=jnp.float32)]
    ppermute x0 -> x3, starting transfers between devices: none -> 3.54 us  [body(): lax.ppermute(summed, 'expert', [(i, (i + k) % groups) for i in range(grou...]
  transfers between devices with their start and end apart: 7 -> 9, of which waited for: 5 -> 6; matrix products, arithmetic and copies ran while one was open for 10% -> 10% of each run, Pallas kernels for 25% -> 26%
where the time goes in v2:
time: 229 us; the launch traced here: 228 us
  waiting for transfers between devices  95.3 us (42%)
  Pallas kernels  60.2 us (26%)
  other arithmetic  17.8 us (8%)
  starting transfers between devices  16.3 us (7%)
  matrix products  14.6 us (6%)
  between operations  14 us (6%)
  local copies, waits for them, and re-layouts  10.1 us (4%)
    all_gather x1, waiting for transfers between devices, body(): gathered = lax.all_gather(arranged, 'seq', axis=1, tiled=True)  55.6 us
    pallas_call x4, Pallas kernels, weight_grads(): pl.pallas_call(kernel, grid=(width // tile,), in_specs=[pl.BlockSpec((1,...  32.8 us
    pallas_call x2, Pallas kernels, expert_terms(): pl.pallas_call(terms_kernel, grid=(hidden // tile,), in_specs=[pl.BlockSp...  27.4 us
    ppermute x3, waiting for transfers between devices, body(): lax.ppermute(summed, 'expert', [(i, (i + k) % groups) for i in range(grou...  15.5 us
    dot_general x8, matrix products, mm(): return lax.dot_general(a, b, dims, preferred_element_type=jnp.float32)  13 us
    all_to_all x1, waiting for transfers between devices, body(): lax.all_to_all(picked.reshape(groups, block, width), 'expert', split_axis...  9.4 us
    all_to_all x1, waiting for transfers between devices, body(): lax.all_to_all(carries, 'seq', split_axis=0, concat_axis=1, tiled=True)  7.94 us
    all_to_all x1, waiting for transfers between devices, body(): lax.all_to_all(sent, 'seq', split_axis=1, concat_axis=0, tiled=True)  6.85 us
  transfers between devices with their start and end apart: 9, of which 6 were waited for; matrix products, arithmetic and copies ran while one was open for 10% of the time, Pallas kernels for 26%

profile of v2, /device:TPU:0, one launch (start us, length us, event | category | flops | bytes accessed | tf_op | source)
XLA Modules:
  0.0 228.2 jit_solution(10656060056343134760)
XLA Ops:
  7.2 1.0 convert_reduce_fusion.1
  8.2 0.7 broadcast_add_fusion
  8.9 0.1 pad_add_fusion
  8.9 2.2 convolution_convert_fusion.2
  11.1 5.2 %all-to-all-start = ((bf16[4,40,2048]{2,1,0:T(8,128)(2,1)}), bf16[4,40,2048]{2,1,0:T(8,128)(2,1)S(1)}, u32[]{:S(2)}, u32[]{:S(2)}) async-start(bf16[4,40,2048]{2,1,0:T(8,128)(2,1)} %bitcast.3), calls=%async_computation | async-start | bytes 1310720 | tf_op jit(solution)/shard_map/all_to_all | solution.py:145
  16.3 9.4 %all-to-all-done = bf16[4,40,2048]{2,1,0:T(8,128)(2,1)S(1)} async-done(((bf16[4,40,2048]{2,1,0:T(8,128)(2,1)}), bf16[4,40,2048]{2,1,0:T(8,128)(2,1)S(1)}, u32[]{:S(2)}, u32[]{:S(2)}) %all-to-all-start) | async-done | bytes 655392 | tf_op jit(solution)/shard_map/all_to_all | solution.py:145
  25.7 1.2 convolution_convert_fusion.1
  27.1 0.7 pad_maximum_fusion.1
  27.8 55.6 %all-gather.3.cloned.1.call-done.x_ref.dy_ref.refs_0_.refs_1_ = bf16[4,320,2048]{2,1,0:T(8,128)(2,1)} async-done(((bf16[4,40,2048]{2,1,0:T(8,128)(2,1)}), bf16[4,320,2048]{2,1,0:T(8,128)(2,1)}) %all-gather.3.cloned.1.call-update) | async-done | bytes 5242896 | tf_op jit(solution)/shard_map/all_gather | solution.py:152
  83.5 13.6 %expert_terms.3 = (bf16[320,1024]{1,0:T(8,128)(2,1)}, bf16[320,1024]{1,0:T(8,128)(2,1)}, bf16[320,1024]{1,0:T(8,128)(2,1)}, bf16[320,2048]{1,0:T(8,128)(2,1)}) custom-call(bf16[4,320,2048]{2,1,0:T(8,128)(2,1)} %all-gather.3.cloned.1.call-done.x_ref.dy_ref.refs_0_.refs_1_, bf16[4,320,2048]{2,1,0:T(8,128)(2,1)} %all-gather.3.cloned.1.call-done.x_ref.dy_ref.refs_0_.refs_1_, ...), custom_call_target="tpu_custom_call" | custom-call | flops 6710886400 | bytes 16515072 | tf_op jit(solution)/shard_map/expert_terms/pallas_call | solution.py:57
  97.1 13.7 %expert_terms.2 = (bf16[320,1024]{1,0:T(8,128)(2,1)}, bf16[320,1024]{1,0:T(8,128)(2,1)}, bf16[320,1024]{1,0:T(8,128)(2,1)}, bf16[320,2048]{1,0:T(8,128)(2,1)}) custom-call(bf16[4,320,2048]{2,1,0:T(8,128)(2,1)} %all-gather.3.cloned.1.call-done.x_ref.dy_ref.refs_0_.refs_1_, bf16[4,320,2048]{2,1,0:T(8,128)(2,1)} %all-gather.3.cloned.1.call-done.x_ref.dy_ref.refs_0_.refs_1_, ...), custom_call_target="tpu_custom_call" | custom-call | flops 6710886400 | bytes 16515072 | tf_op jit(solution)/shard_map/expert_terms/pallas_call | solution.py:57
  110.9 3.0 %pad_maximum_fusion = bf16[8,2,40,2048]{3,2,1,0:T(8,128)(2,1)} fusion(bf16[8,1,40,2048]{3,2,1,0:T(8,128)(2,1)S(1)} %bitcast.166, bf16[8,1,40,2048]{3,2,1,0:T(8,128)(2,1)} %bitcast.167), kind=kLoop, calls=%fused_computation.1 | loop fusion | flops 1310720 | bytes 5242880 | tf_op jit(solution)/shard_map/stack | solution.py:161
  113.9 0.7 copy-done.8
  114.6 0.6 reduce-window.6
  115.2 0.2 slice_reduce_fusion
  115.5 0.1 broadcast_in_dim.92
  115.6 0.3 copy.71
  115.9 0.1 exp.10
  116.1 0.2 slice_reduce_fusion.1
  116.4 1.2 subtract_exponential_fusion
  117.6 0.6 slice.226
  118.2 0.7 pad.3.clone
  118.8 0.6 and_select_fusion.4
  119.5 0.6 subtract_convert_fusion
  120.1 0.2 convolution_select_fusion
  120.3 1.0 multiply_convert_fusion
  121.3 6.6 %weight_grads.6.refs_2_ = f32[2,1024,2048]{2,1,0:T(8,128)} custom-call(bf16[1,320,1024]{2,1,0:T(8,128)(2,1)} %bitcast.170, bf16[4,320,2048]{2,1,0:T(8,128)(2,1)} %all-gather.3.cloned.1.call-done.x_ref.dy_ref.refs_0_.refs_1_), custom_call_target="tpu_custom_call" | custom-call | flops 1342177280 | bytes 8388608 | tf_op jit(solution)/shard_map/weight_grads/pallas_call | solution.py:94
  127.9 6.7 %weight_grads.7 = f32[2,1024,2048]{2,1,0:T(8,128)} custom-call(bf16[1,320,1024]{2,1,0:T(8,128)(2,1)} %bitcast.173, bf16[4,320,2048]{2,1,0:T(8,128)(2,1)} %all-gather.3.cloned.1.call-done.x_ref.dy_ref.refs_0_.refs_1_, f32[2,1024,2048]{2,1,0:T(8,128)} %weight_grads.6.refs_2_), custom_call_target="tpu_custom_call", output_to_operand_aliasing={{}: (2, {})} | custom-call | flops 1342177280 | bytes 8388608 | tf_op jit(solution)/shard_map/weight_grads/pallas_call | solution.py:94
  134.5 9.8 %weight_grads.4 = (f32[2,2048,1024]{2,1,0:T(8,128)}, f32[2,2048,1024]{2,1,0:T(8,128)}) custom-call(bf16[4,320,2048]{2,1,0:T(8,128)(2,1)} %all-gather.3.cloned.1.call-done.x_ref.dy_ref.refs_0_.refs_1_, bf16[1,320,1024]{2,1,0:T(8,128)(2,1)} %bitcast.179, bf16[1,320,1024]{2,1,0:T(8,128)(2,1)} %bitcast.180), custom_call_target="tpu_custom_call" | custom-call | flops 2684354560 | bytes 16777216 | tf_op jit(solution)/shard_map/weight_grads/pallas_call | solution.py:94
  144.3 9.8 %weight_grads.5 = (f32[2,2048,1024]{2,1,0:T(8,128)}, f32[2,2048,1024]{2,1,0:T(8,128)}) custom-call(bf16[4,320,2048]{2,1,0:T(8,128)(2,1)} %all-gather.3.cloned.1.call-done.x_ref.dy_ref.refs_0_.refs_1_, bf16[1,320,1024]{2,1,0:T(8,128)(2,1)} %bitcast.171, bf16[1,320,1024]{2,1,0:T(8,128)(2,1)} %bitcast.172, ...), custom_call_target="tpu_custom_call", output_to_operand_aliasing={{0}: (3, {}), {1}: (4, {})} | custom-call | flops 2684354560 | bytes 16777216 | tf_op jit(solution)/shard_map/weight_grads/pallas_call | solution.py:94
  154.1 1.5 slice.116
  155.6 0.9 copy.77
  156.5 4.8 %fusion.12 = f32[256,1024]{1,0:T(8,128)} fusion(bf16[1024,2048]{1,0:T(8,128)(2,1)} %param.16, bf16[256,2176]{1,0:T(8,128)(2,1)} %all-gather.5.cloned.1.call-done), kind=kOutput, calls=%fused_computation.21 | convolution fusion | flops 1073741824 | bytes 6291456 | tf_op jit(solution)/shard_map/dot_general | solution.py:17
  161.3 2.4 %collective-permute-start.2 = (bf16[80,2048]{1,0:T(8,128)(2,1)}, bf16[80,2048]{1,0:T(8,128)(2,1)S(1)}, u32[]{:S(2)}, u32[]{:S(2)}) collective-permute-start(bf16[80,2048]{1,0:T(8,128)(2,1)} %bitcast.181), channel_id=1, source_target_pairs={{0,24},{8,0},{16,8},{24,16},{1,25},{9,1},{17,9},{25,17},{2,26},{10... | collective-permute-start | bytes 983048 | tf_op jit(solution)/shard_map/ppermute | solution.py:195
  163.7 0.5 collective-permute-start.1
  164.3 0.6 collective-permute-start
  164.8 0.2 convert_reduce_fusion
  165.1 7.1 %collective-permute-done.2 = bf16[80,2048]{1,0:T(8,128)(2,1)S(1)} collective-permute-done((bf16[80,2048]{1,0:T(8,128)(2,1)}, bf16[80,2048]{1,0:T(8,128)(2,1)S(1)}, u32[]{:S(2)}, u32[]{:S(2)}) %collective-permute-start.2) | collective-permute-done | bytes 327712 | tf_op jit(solution)/shard_map/ppermute | solution.py:195
  172.1 8.4 %collective-permute-done.1 = bf16[80,2048]{1,0:T(8,128)(2,1)S(1)} collective-permute-done((bf16[80,2048]{1,0:T(8,128)(2,1)}, bf16[80,2048]{1,0:T(8,128)(2,1)S(1)}, u32[]{:S(2)}, u32[]{:S(2)}) %collective-permute-start.1) | collective-permute-done | bytes 327712 | tf_op jit(solution)/shard_map/ppermute | solution.py:195
  180.6 1.9 convolution_convert_fusion
  182.5 0.4 copy-done.12
  182.9 0.3 copy-done.13
  183.2 2.2 fusion.67
  185.4 0.3 fusion.11
  185.7 0.8 copy_bitcast_fusion
  186.5 4.1 %all-to-all-start.1 = ((bf16[144,8,128]{2,0,1:T(8,128)(2,1)}), bf16[144,8,128]{2,0,1:T(8,128)(2,1)}, u32[]{:S(2)}, u32[]{:S(2)}) async-start(bf16[144,8,128]{2,0,1:T(8,128)(2,1)} %copy_bitcast_fusion), calls=%async_computation.2 | async-start | bytes 589824 | tf_op jit(solution)/shard_map/all_to_all | solution.py:211
  190.6 2.1 copy.73
  192.7 1.5 fusion.68
  194.2 6.8 %all-to-all-done.1 = bf16[144,8,128]{2,0,1:T(8,128)(2,1)} async-done(((bf16[144,8,128]{2,0,1:T(8,128)(2,1)}), bf16[144,8,128]{2,0,1:T(8,128)(2,1)}, u32[]{:S(2)}, u32[]{:S(2)}) %all-to-all-start.1) | async-done | bytes 294944 | tf_op jit(solution)/shard_map/all_to_all | solution.py:211
  201.0 1.0 convert_bitcast_fusion
  202.1 0.7 fusion.36
  202.7 0.6 convert_dynamic-update-slice_fusion.4
  203.3 0.6 convert_dynamic-update-slice_fusion.3
  204.0 0.6 convert_dynamic-update-slice_fusion.2
  204.6 0.6 convert_dynamic-update-slice_fusion.1
  205.2 0.6 convert_dynamic-update-slice_fusion
  205.8 0.6 fusion.35
  206.5 0.6 constant_dynamic-update-slice_fusion
  207.1 3.4 %all-to-all-start.2 = ((bf16[8,128,128]{2,1,0:T(8,128)(2,1)}), bf16[8,128,128]{2,1,0:T(8,128)(2,1)S(1)}, u32[]{:S(2)}, u32[]{:S(2)}) async-start(bf16[8,128,128]{2,1,0:T(8,128)(2,1)} %bitcast.44), calls=%async_computation.3 | async-start | bytes 524288 | tf_op jit(solution)/shard_map/all_to_all | solution.py:226
  210.5 1.7 fusion.17
  212.2 7.9 %all-to-all-done.2 = bf16[8,128,128]{2,1,0:T(8,128)(2,1)S(1)} async-done(((bf16[8,128,128]{2,1,0:T(8,128)(2,1)}), bf16[8,128,128]{2,1,0:T(8,128)(2,1)S(1)}, u32[]{:S(2)}, u32[]{:S(2)}) %all-to-all-start.2) | async-done | bytes 262176 | tf_op jit(solution)/shard_map/all_to_all | solution.py:226
  220.2 0.2 copy.75
  220.4 0.3 fusion.10
  220.7 1.0 copy.76
  (50 shorter events, 0.7 us)
Async XLA Ops:
  7.2 112.9 %copy-start = (bf16[1,256,128]{2,1,0:T(8,128)(2,1)S(1)}, bf16[1,256,128]{2,1,0:T(8,128)(2,1)}, u32[]{:S(2)}) copy-start(bf16[1,256,128]{2,1,0:T(8,128)(2,1)} %param.17) | copy-start | bytes 196612
  7.2 19.8 %copy-start.9 = (s32[1,64,1]{1,2,0:T(1,128)S(1)}, s32[1,64,1]{1,2,0:T(1,128)}, u32[]{:S(2)}) copy-start(s32[1,64,1]{1,2,0:T(1,128)} %param.12) | copy-start | bytes 772
  7.2 19.9 %copy-start.2 = (bf16[1,64,2048]{2,1,0:T(8,128)(2,1)S(1)}, bf16[1,64,2048]{2,1,0:T(8,128)(2,1)}, u32[]{:S(2)}) copy-start(bf16[1,64,2048]{2,1,0:T(8,128)(2,1)} %param.11) | copy-start | bytes 786436
  11.1 14.6 %all-to-all-start = ((bf16[4,40,2048]{2,1,0:T(8,128)(2,1)}), bf16[4,40,2048]{2,1,0:T(8,128)(2,1)S(1)}, u32[]{:S(2)}, u32[]{:S(2)}) async-start(bf16[4,40,2048]{2,1,0:T(8,128)(2,1)} %bitcast.3), calls=%async_computation | async-start | bytes 1310720 | tf_op jit(solution)/shard_map/all_to_all | solution.py:145
  16.3 67.1 %all-gather.3.cloned.1.call-start = ((), (), s32[]{:S(2)}) async-start(), calls=%async_computation.4 | async-start | bytes 5898240 | tf_op jit(solution)/shard_map/all_gather | solution.py:152
  27.0 127.1 %all-gather.5.cloned.1.call-start = ((), (), s32[]{:S(2)}) async-start(), calls=%async_computation.6 | async-start | bytes 1392640 | tf_op jit(solution)/shard_map/all_gather | solution.py:158
  83.4 77.9 %reduce-scatter.2.cloned.1.call-start = ((), (), s32[]{:S(2)}) async-start(), calls=%async_computation.5 | async-start | bytes 2949120 | tf_op jit(solution)/shard_map/reduce_scatter | solution.py:162
  97.1 13.7 %copy-start.3 = (bf16[320,2048]{1,0:T(8,128)(2,1)S(1)}, bf16[320,2048]{1,0:T(8,128)(2,1)}, u32[]{:S(2)}) copy-start(bf16[320,2048]{1,0:T(8,128)(2,1)} %get-tuple-element.29) | copy-start | bytes 3932164
  113.9 0.7 copy-start.8
  115.6 4.5 %copy-start.4 = (bf16[1,256,128]{2,1,0:T(8,128)(2,1)S(1)}, bf16[1,256,128]{2,1,0:T(8,128)(2,1)}, u32[]{:S(2)}) copy-start(bf16[1,256,128]{2,1,0:T(8,128)(2,1)} %param.18) | copy-start | bytes 196612
  156.5 8.4 %copy-start.10 = (s32[256]{0:T(256)S(1)}, s32[256]{0:T(256)}, u32[]{:S(2)}) copy-start(s32[256]{0:T(256)} %and_select_fusion.4) | copy-start | bytes 3076
  161.3 10.8 %collective-permute-start.2 = (bf16[80,2048]{1,0:T(8,128)(2,1)}, bf16[80,2048]{1,0:T(8,128)(2,1)S(1)}, u32[]{:S(2)}, u32[]{:S(2)}) collective-permute-start(bf16[80,2048]{1,0:T(8,128)(2,1)} %bitcast.181), channel_id=1, source_target_pairs={{0,24},{8,0},{16,8},{24,16},{1,25},{9,1},{17,9},{25,17},{2,26},{10... | collective-permute-start | bytes 983048 | tf_op jit(solution)/shard_map/ppermute | solution.py:195
  163.7 16.8 %collective-permute-start.1 = (bf16[80,2048]{1,0:T(8,128)(2,1)}, bf16[80,2048]{1,0:T(8,128)(2,1)S(1)}, u32[]{:S(2)}, u32[]{:S(2)}) collective-permute-start(bf16[80,2048]{1,0:T(8,128)(2,1)} %bitcast.182), channel_id=1, source_target_pairs={{0,16},{8,24},{16,0},{24,8},{1,17},{9,25},{17,1},{25,9},{2,18},{10... | collective-permute-start | bytes 983048 | tf_op jit(solution)/shard_map/ppermute | solution.py:195
  164.3 16.3 %collective-permute-start = (bf16[80,2048]{1,0:T(8,128)(2,1)}, bf16[80,2048]{1,0:T(8,128)(2,1)S(1)}, u32[]{:S(2)}, u32[]{:S(2)}) collective-permute-start(bf16[80,2048]{1,0:T(8,128)(2,1)} %bitcast.183), channel_id=1, source_target_pairs={{0,8},{8,16},{16,24},{24,0},{1,9},{9,17},{17,25},{25,1},{2,10},{10... | collective-permute-start | bytes 983048 | tf_op jit(solution)/shard_map/ppermute | solution.py:195
  180.6 2.3 %copy-start.12 = (bf16[1024,2048]{1,0:T(8,128)(2,1)S(1)}, bf16[1024,2048]{1,0:T(8,128)(2,1)}, u32[]{:S(2)}) copy-start(bf16[1024,2048]{1,0:T(8,128)(2,1)} %param.16) | copy-start | bytes 12582916
  180.6 2.6 %copy-start.13 = (f32[256,1024]{1,0:T(8,128)S(1)}, f32[256,1024]{1,0:T(8,128)}, u32[]{:S(2)}) copy-start(f32[256,1024]{1,0:T(8,128)} %fusion.12) | copy-start | bytes 3145732
  183.2 2.2 copy-start.5
  183.2 2.5 %copy-start.6 = (bf16[1,1024]{1,0:T(2,128)(2,1)S(1)}, bf16[1,1024]{1,0:T(2,128)(2,1)}, u32[]{:S(2)}) copy-start(bf16[1,1024]{1,0:T(2,128)(2,1)} %slice.226) | copy-start | bytes 6148
  183.2 2.5 %copy-start.7 = (bf16[1,1024]{1,0:T(2,128)(2,1)S(1)}, bf16[1,1024]{1,0:T(2,128)(2,1)}, u32[]{:S(2)}) copy-start(bf16[1,1024]{1,0:T(2,128)(2,1)} %subtract_convert_fusion) | copy-start | bytes 6148
  183.2 2.5 %copy-start.11 = (bf16[144]{0:T(256)(128)(2,1)S(1)}, bf16[144]{0:T(256)(128)(2,1)}, u32[]{:S(2)}) copy-start(bf16[144]{0:T(256)(128)(2,1)} %pad.3.clone) | copy-start | bytes 868
  186.5 14.5 %all-to-all-start.1 = ((bf16[144,8,128]{2,0,1:T(8,128)(2,1)}), bf16[144,8,128]{2,0,1:T(8,128)(2,1)}, u32[]{:S(2)}, u32[]{:S(2)}) async-start(bf16[144,8,128]{2,0,1:T(8,128)(2,1)} %copy_bitcast_fusion), calls=%async_computation.2 | async-start | bytes 589824 | tf_op jit(solution)/shard_map/all_to_all | solution.py:211
  194.2 26.2 %copy-start.1 = (f32[256,1024]{0,1:T(8,128)S(1)}, f32[256,1024]{0,1:T(8,128)}, u32[]{:S(2)}) copy-start(f32[256,1024]{0,1:T(8,128)} %subtract_exponential_fusion) | copy-start | bytes 3145732
  207.1 13.1 %all-to-all-start.2 = ((bf16[8,128,128]{2,1,0:T(8,128)(2,1)}), bf16[8,128,128]{2,1,0:T(8,128)(2,1)S(1)}, u32[]{:S(2)}, u32[]{:S(2)}) async-start(bf16[8,128,128]{2,1,0:T(8,128)(2,1)} %bitcast.44), calls=%async_computation.3 | async-start | bytes 524288 | tf_op jit(solution)/shard_map/all_to_all | solution.py:226
Sparse Core Ops, SparseCore 0:
  27.1 56.2 all-gather.2
  85.8 25.9 all-gather.4
  114.2 37.5 reduce-scatter.1
